TPU v7x, 32 devices: a whole 2x2x4 slice. The times are simulated.
32 devices in a mesh: groups: 2 (over y), orient: 4 (over z), cls: 2 (over x), dom: 2 (over core).
Axes of the slice: x: 2, y: 2, z: 4, core: 2. Of those that a mesh axis runs over, the one named last changes fastest.
Arguments:
- particles: bfloat16 [256, 2, 16512], P(('groups', 'orient', 'cls', 'dom')), parts along dimension 0, may hold values from -10 to 10
- ctf_index: int32 [256], P(('groups', 'orient', 'cls', 'dom')), parts along dimension 0, may hold values from 0 to 15
- beta: bfloat16 [256], P(('groups', 'orient', 'cls', 'dom')), parts along dimension 0, may hold values from 10 to 60
- significant: int32 [128, 1], P(('groups', 'orient', 'cls', 'dom')), parts along dimension 0, may hold values from 0 to 3; in each aligned block of 4 rows (0 to 3, 4 to 7, ...) at most 2 rows name the same one
- ctf_table: bfloat16 [16, 16512], replicated, may hold values from 0.049804688 to 1
- references: bfloat16 [4, 4, 4, 2, 16512], P(('groups', 'cls'), 'orient'), parts along dimension 0, may hold values from -4 to 4
- offsets: int32 [10, 2], P('groups'), parts along dimension 0, may hold values from -3 to 3, as said below
Outputs:
- class_post: float32 [256, 2], P(('groups', 'orient', 'cls', 'dom')), parts along dimension 0
- log_evidence: float32 [256], P(('groups', 'orient', 'cls', 'dom')), parts along dimension 0
There are 2 independent parts, one for each index of `groups`. A program takes and returns all parts, laid end to end along the dimension named above; an argument that names none is the same for every part. Nothing has to cross between parts.
Inputs may be any that keep to these rules, and one draw needn't show every extreme that they name: `significant`: each block of 2 particles names 1 different orientation groups; the 4 blocks of one device name any one group at most 2 times. The 5 offsets are distinct pairs.
All inputs are finite; a program needn't handle non-finite values.
Results may differ from a plain program's by a relative error of at most 0.0003.
Values may be sent and summed in bfloat16 or wider, within the bound.
A program may use at most 128 MiB of HBM per device.

v0:
```python
import math

import jax
import jax.numpy as jnp
from jax import lax
from jax.sharding import PartitionSpec as P

BOX = 256
KX = 129
KY = 128


EPSILON = 1e-06


def phase_tables(offsets):
    pixel_index = jnp.arange(KX * KY, dtype=jnp.int32)
    freq_x = pixel_index % KX
    freq_y = pixel_index // KX - KY // 2
    phase_rotations = jnp.mod(
        offsets[:, 0:1] * freq_x[None, :] + offsets[:, 1:2] * freq_y[None, :], BOX
    )
    angles = phase_rotations.astype(jnp.float32) * (2.0 * math.pi / BOX)
    return (jnp.cos(angles), jnp.sin(angles))


def shifted_table(refs_now, cosines, sines):
    real_part = refs_now[:, 0, :].astype(jnp.float32)
    imag_part = refs_now[:, 1, :].astype(jnp.float32)
    translation_real = real_part[None] * cosines[:, None] + imag_part[None] * sines[:, None]
    shift_imag = imag_part[None] * cosines[:, None] - real_part[None] * sines[:, None]
    shifted = jnp.stack([translation_real, shift_imag], axis=2).astype(jnp.bfloat16)
    return shifted.reshape(shifted.shape[0] * shifted.shape[1], 2 * shifted.shape[3])


def ref_energy(refs_now):
    return jnp.sum(jnp.square(refs_now.astype(jnp.float32)), axis=1)


def class_evidence(weighted, image_power, inverse_noise, power_of, refs_now, cosines, sines):
    shifted = shifted_table(refs_now, cosines, sines)
    intersection = lax.dot_general(
        weighted, shifted, (((1,), (1,)), ((), ())), preferred_element_type=jnp.float32
    )
    ref_power = power_of(ref_energy(refs_now))
    orients = refs_now.shape[0]
    intersection = intersection.reshape(intersection.shape[0], -1, orients)
    normalizer = jnp.sqrt(image_power[:, None] * ref_power + EPSILON)
    logits = inverse_noise[:, None, None] * intersection / normalizer[:, None, :]
    return jnp.sum(jnp.exp(logits), axis=(1, 2))


def local(particles, ctf_index, beta, significant, ctf_table, references, offsets):
    groups = lax.axis_size("orient")
    blocks = significant.shape[0]
    listed_count = significant.shape[1]
    per_block = particles.shape[0] // blocks
    pixels = particles.shape[2]
    ctf_codes = ctf_table.shape[0]
    capacity = max(2, 2 * blocks * listed_count // groups)
    cosines, sines = phase_tables(offsets)
    member_entry = jnp.any(
        significant[:, :, None] == jnp.arange(groups, dtype=jnp.int32)[None, None, :], axis=1
    ).astype(jnp.int32)
    slot_rank = jnp.cumsum(member_entry, axis=0) - member_entry
    placed = member_entry[:, :, None] * (
        slot_rank[:, :, None] == jnp.arange(capacity, dtype=jnp.int32)[None, None, :]
    ).astype(jnp.int32)
    routing = (
        jnp.transpose(placed, (1, 2, 0)).reshape(groups * capacity, blocks).astype(jnp.float32)
    )
    routing_half = routing.astype(jnp.bfloat16)

    def dispatch(values):
        flattened = values.reshape(blocks, -1)
        dispatched = jnp.dot(routing_half, flattened, preferred_element_type=jnp.float32).astype(
            jnp.bfloat16
        )
        return dispatched.reshape((groups, capacity * per_block) + values.shape[2:])

    particle_blocks = dispatch(particles.reshape(blocks, per_block, 2, pixels))
    extras = jnp.stack([ctf_index.astype(jnp.bfloat16), beta], axis=1)
    outgoing = (particle_blocks, dispatch(extras.reshape(blocks, per_block, 2)))

    def prepare(received):
        particle_images = received[0]
        slot_count = particle_images.shape[0] * particle_images.shape[1]
        flattened = particle_images.reshape(slot_count, 2, pixels)
        image_power = jnp.sum(jnp.square(flattened.astype(jnp.float32)), axis=(1, 2))
        extras = received[1].reshape(slot_count, 2)
        ctf_select = (
            extras[:, 0:1].astype(jnp.float32) == jnp.arange(ctf_codes, dtype=jnp.float32)[None, :]
        ).astype(jnp.float32)
        inverse_noise = extras[:, 1].astype(jnp.float32)
        ctf_rows = jnp.dot(
            ctf_select.astype(jnp.bfloat16), ctf_table, preferred_element_type=jnp.float32
        ).astype(jnp.bfloat16)
        table_squares = jnp.square(ctf_table.astype(jnp.float32))

        def power_of(energy):
            table_power = lax.dot_general(
                table_squares,
                energy,
                (((1,), (1,)), ((), ())),
                precision=lax.Precision.HIGHEST,
                preferred_element_type=jnp.float32,
            )
            return jnp.dot(
                ctf_select,
                table_power,
                precision=lax.Precision.HIGHEST,
                preferred_element_type=jnp.float32,
            )

        weighted = (
            ctf_rows.astype(jnp.float32)[:, None, :] * flattened.astype(jnp.float32)
        ).astype(jnp.bfloat16)
        return (
            weighted.reshape(slot_count, 2 * pixels),
            image_power,
            inverse_noise,
            power_of,
            slot_count,
        )

    every_class = lax.all_gather(references, "cls", axis=0, tiled=True)
    received = (
        lax.all_to_all(outgoing[0], "orient", split_axis=0, concat_axis=0, tiled=True),
        lax.all_to_all(outgoing[1], "orient", split_axis=0, concat_axis=0, tiled=True),
    )
    weighted, image_power, inverse_noise, power_of, slot_count = prepare(received)
    columns = [
        class_evidence(
            weighted, image_power, inverse_noise, power_of, every_class[class_id, 0], cosines, sines
        )
        for class_id in range(every_class.shape[0])
    ]
    marginal_evidence = jnp.stack(columns, axis=1)
    shaped = marginal_evidence.reshape(
        received[0].shape[0], received[0].shape[1], marginal_evidence.shape[1]
    )
    returned = lax.all_to_all(shaped, "orient", split_axis=0, concat_axis=0, tiled=True)
    class_total = returned.shape[2]
    returned_rows = returned.reshape(groups * capacity, per_block * class_total)
    home_sums = lax.dot_general(
        routing,
        returned_rows,
        (((0,), (0,)), ((), ())),
        precision=lax.Precision.HIGHEST,
        preferred_element_type=jnp.float32,
    )
    evidence_home = home_sums.reshape(blocks * per_block, class_total)
    all_classes = jnp.sum(evidence_home, axis=1)
    return (evidence_home / all_classes[:, None], jnp.log(all_classes))


def solution(mesh):
    placed = (
        P(("groups", "orient", "cls", "dom"), None, None),
        P(("groups", "orient", "cls", "dom")),
        P(("groups", "orient", "cls", "dom")),
        P(("groups", "orient", "cls", "dom"), None),
        P(),
        P(("groups", "cls"), "orient", None, None, None),
        P("groups", None),
    )
    return jax.shard_map(
        local,
        mesh=mesh,
        in_specs=placed,
        out_specs=(
            P(("groups", "orient", "cls", "dom"), None),
            P(("groups", "orient", "cls", "dom")),
        ),
        check_vma=False,
    )
```

profile of v0, /device:TPU:0, one launch (start us, length us, event | category | flops | bytes accessed | tf_op | source)
XLA Modules:
  0.0 75.0 jit_solution(8348397335872190462)
XLA Ops:
  0.6 0.7 fusion.67
  1.4 0.7 fusion.66
  2.2 0.7 bitcast_subtract_fusion
  2.9 0.7 convert_bitcast_fusion
  3.5 0.7 pad_maximum_fusion.1
  4.7 0.7 copy.23
  5.4 6.3 %all-to-all-start = ((bf16[4,4,2]{1,2,0:T(2,128)(2,1)}), bf16[4,4,2]{1,2,0:T(2,128)(2,1)S(1)}, u32[]{:S(2)}, u32[]{:S(2)}) async-start(bf16[4,4,2]{1,2,0:T(2,128)(2,1)} %copy.23), calls=%async_computation | async-start | bytes 4096 | tf_op jit(solution)/shard_map/all_to_all | solution.py:129
  12.4 0.8 %slice_bitcast_fusion.7 = (s32[5]{0:T(128)S(1)}, s32[5]{0:T(128)S(1)}) fusion(s32[5,2]{0,1:T(2,128)} %param.13), kind=kLoop, calls=%fused_computation.88 | loop fusion | bytes 80 | tf_op jit(solution)/shard_map/mul | solution.py:21
  13.2 1.1 %copy.26 = bf16[1,1,4,2,16512]{4,2,3,1,0:T(4,128)(2,1)S(1)} copy(bf16[1,1,4,2,16512]{4,3,2,1,0:T(2,128)(2,1)} %param.12) | data formatting | bytes 528384 | tf_op args[5]
  14.2 8.5 %all_gather.3 = bf16[2,1,4,2,16512]{4,2,3,1,0:T(4,128)(2,1)S(1)} all-gather(bf16[1,1,4,2,16512]{4,2,3,1,0:T(4,128)(2,1)S(1)} %copy.26), channel_id=1, replica_groups=mesh['groups'=2,'orient'=4,'cls'=2,'dom'=2] {'cls'}, dimensions={0}, use_global_device_ids=true | all-gather | bytes 792576 | tf_op jit(solution)/shard_map/all_gather | solution.py:126
  23.7 0.9 %fusion.53 = (f32[4,16512]{1,0:T(4,128)S(1)}, f32[4,16512]{1,0:T(4,128)}, f32[4,16512]{1,0:T(4,128)}, f32[4,16512]{1,0:T(4,128)}) fusion(bf16[4,2,16512]{2,0,1:T(4,128)(2,1)S(1)} %get-tuple-element.17, bf16[4,2,16512]{2,0,1:T(4,128)(2,1)S(1)} %get-tuple-element.16), kind=kLoop, calls=%fused_computation.54 | loop fusion | flops 264192 | bytes 1585152 | tf_op jit(solution)/shard_map/convert_element_type | solution.py:28
  24.6 2.2 %fusion.51 = (f32[5,16512]{1,0:T(8,128)S(1)}, f32[5,16512]{1,0:T(8,128)S(1)}) fusion(s32[16512]{0:T(1024)S(1)} %copy-done.4, s32[5]{0:T(128)S(1)} %get-tuple-element.27, s32[16512]{0:T(1024)S(1)} %get-tuple-element.30, s32[5]{0:T(128)S(1)} %get-tuple-element.26), kind=kLoop, calls=%fused_computation.48 | loop fusion | flops 1320960 | bytes 792616 | tf_op jit(solution)/shard_map/cos | solution.py:24
  26.8 1.3 %reshape.429 = bf16[4,4,2,16512]{3,2,1,0:T(2,128)(2,1)} reshape(bf16[8,66048]{1,0:T(8,128)(2,1)S(1)} %convolution_convert_fusion) | data formatting | bytes 2113536 | tf_op jit(solution)/shard_map/reshape | solution.py:79
  28.0 4.8 %all-to-all-start.1 = ((bf16[4,4,2,16512]{3,2,1,0:T(2,128)(2,1)}), bf16[4,4,2,16512]{3,2,1,0:T(2,128)(2,1)S(1)}, u32[]{:S(2)}, u32[]{:S(2)}) async-start(bf16[4,4,2,16512]{3,2,1,0:T(2,128)(2,1)} %reshape.429), calls=%async_computation.1 | async-start | bytes 2113536 | tf_op jit(solution)/shard_map/all_to_all | solution.py:128
  32.8 3.6 %add_convert_fusion.1 = (bf16[5,4,1,16512]{3,0,2,1:T(8,128)(2,1)}, bf16[5,4,1,16512]{3,0,2,1:T(8,128)(2,1)}, bf16[5,4,1,16512]{3,0,2,1:T(8,128)(2,1)}, bf16[5,4,1,16512]{3,0,2,1:T(8,128)(2,1)}) fusion(f32[5,16512]{1,0:T(8,128)S(1)} %get-tuple-element.23, f32[4,16512]{1,0:T(4,128)} %get-tuple-element.32, f32[5,16512]{1,0:T(8,128)S(1)} %get-tuple-element.22, ...), kind=kLoop, calls=%fused_computation.17 | loop fusion | flops 5283840 | bytes 4359168 | tf_op jit(solution)/shard_map/convert.9
  36.8 1.4 %fusion.45 = f32[16,4]{0,1:T(4,128)S(1)} fusion(f32[4,16512]{1,0:T(4,128)S(1)} %get-tuple-element.9, bf16[16,16512]{1,0:T(8,128)(2,1)S(1)} %copy-done), kind=kOutput, calls=%fused_computation.37 | convolution fusion | flops 13209600 | bytes 792832 | tf_op jit(solution)/shard_map/dot_general | solution.py:101
  38.2 1.4 %fusion.46 = f32[16,4]{0,1:T(4,128)S(1)} fusion(f32[4,16512]{1,0:T(4,128)S(1)} %get-tuple-element.8, bf16[16,16512]{1,0:T(8,128)(2,1)S(1)} %copy-done), kind=kOutput, calls=%fused_computation.38 | convolution fusion | flops 13209600 | bytes 792832 | tf_op jit(solution)/shard_map/dot_general | solution.py:101
  39.7 1.4 %fusion = f32[16,16512]{1,0:T(8,128)} fusion(bf16[16,16512]{1,0:T(8,128)(2,1)S(1)} %copy-done, f32[16]{0:T(128)S(1)} %get-tuple-element.29), kind=kOutput, calls=%fused_computation.2 | convolution fusion | flops 8983296 | bytes 1585216 | tf_op jit(solution)/shard_map/dot_general | solution.py:95
  41.1 16.1 %all-to-all-done.1 = bf16[4,4,2,16512]{3,2,1,0:T(2,128)(2,1)S(1)} async-done(((bf16[4,4,2,16512]{3,2,1,0:T(2,128)(2,1)}), bf16[4,4,2,16512]{3,2,1,0:T(2,128)(2,1)S(1)}, u32[]{:S(2)}, u32[]{:S(2)}) %all-to-all-start.1) | async-done | bytes 1056800 | tf_op jit(solution)/shard_map/all_to_all | solution.py:128
  57.2 1.2 %multiply_reduce_fusion = f32[4,4]{1,0:T(4,128)S(1)} fusion(bf16[4,4,2,16512]{3,2,1,0:T(2,128)(2,1)S(1)} %all-to-all-done.1), kind=kLoop, calls=%fused_computation.15 | loop fusion | flops 1585136 | bytes 1056832 | tf_op jit(solution)/shard_map/reduce_sum | solution.py:89
  58.8 0.8 %bitcast_convert_fusion.2 = f32[16,2,16512]{2,1,0:T(2,128)S(1)} fusion(bf16[4,4,2,16512]{3,2,1,0:T(2,128)(2,1)S(1)} %all-to-all-done.1), kind=kLoop, calls=%fused_computation.93 | loop fusion | flops 528384 | bytes 3170304 | tf_op jit(solution)/shard_map/convert_element_type | solution.py:116
  59.8 2.5 %fusion.34 = f32[16]{0:T(128)S(1)} fusion(bf16[5,4,1,16512]{3,0,2,1:T(8,128)(2,1)} %get-tuple-element.14, bf16[5,4,1,16512]{3,0,2,1:T(8,128)(2,1)} %get-tuple-element.15, f32[16,4]{0,1:T(4,128)S(1)} %fusion.41, f32[16]{0:T(128)S(1)} %get-tuple-element.28, f32[16,2,16512]{2,1,0:T(2,128)S(1)} %bitcast_convert_fusion.2, f32[16,16512]{1,0:T(8,128)S(1)} %copy-done.1), kind=kOutput, calls=%fused_computation.26 | convolution fusion | flops 24834992 | bytes 4491648 | tf_op jit(solution)/shard_map/dot_general | solution.py:42
  62.6 2.4 %fusion.37 = f32[16]{0:T(128)S(1)} fusion(bf16[5,4,1,16512]{3,0,2,1:T(8,128)(2,1)} %get-tuple-element.11, bf16[5,4,1,16512]{3,0,2,1:T(8,128)(2,1)} %get-tuple-element.10, f32[16,4]{0,1:T(4,128)S(1)} %fusion.43, f32[16]{0:T(128)S(1)} %get-tuple-element.28, f32[16,2,16512]{2,1,0:T(2,128)S(1)} %bitcast_convert_fusion.2, f32[16,16512]{1,0:T(8,128)S(1)} %copy-done.2), kind=kOutput, calls=%fused_computation.27 | convolution fusion | flops 24834992 | bytes 4491648 | tf_op jit(solution)/shard_map/dot_general | solution.py:42
  65.0 8.1 %all_to_all.15 = f32[4,4,2]{1,2,0:T(2,128)S(1)} all-to-all(f32[4,4,2]{1,2,0:T(2,128)S(1)} %copy.27), channel_id=1, replica_groups=mesh['groups'=2,'orient'=4,'cls'=2,'dom'=2] {'orient'}, dimensions={0} | all-to-all | bytes 256 | tf_op jit(solution)/shard_map/all_to_all | solution.py:142
  (41 shorter events, 5.5 us)
Async XLA Ops:
  0.6 22.3 %copy-start.3 = (bf16[8,2,16512]{2,1,0:T(2,128)(2,1)S(1)}, bf16[8,2,16512]{2,1,0:T(2,128)(2,1)}, u32[]{:S(2)}) copy-start(bf16[8,2,16512]{2,1,0:T(2,128)(2,1)} %param.7) | copy-start | bytes 1585156
  5.4 22.6 %all-to-all-start = ((bf16[4,4,2]{1,2,0:T(2,128)(2,1)}), bf16[4,4,2]{1,2,0:T(2,128)(2,1)S(1)}, u32[]{:S(2)}, u32[]{:S(2)}) async-start(bf16[4,4,2]{1,2,0:T(2,128)(2,1)} %copy.23), calls=%async_computation | async-start | bytes 4096 | tf_op jit(solution)/shard_map/all_to_all | solution.py:129
  23.2 1.3 %copy-start.4 = (s32[16512]{0:T(1024)S(1)}, s32[16512]{0:T(1024)}, u32[]{:S(2)}) copy-start(s32[16512]{0:T(1024)} %get-tuple-element.31) | copy-start | bytes 198148
  28.0 29.2 %all-to-all-start.1 = ((bf16[4,4,2,16512]{3,2,1,0:T(2,128)(2,1)}), bf16[4,4,2,16512]{3,2,1,0:T(2,128)(2,1)S(1)}, u32[]{:S(2)}, u32[]{:S(2)}) async-start(bf16[4,4,2,16512]{3,2,1,0:T(2,128)(2,1)} %reshape.429), calls=%async_computation.1 | async-start | bytes 2113536 | tf_op jit(solution)/shard_map/all_to_all | solution.py:128
  32.8 4.0 %copy-start = (bf16[16,16512]{1,0:T(8,128)(2,1)S(1)}, bf16[16,16512]{1,0:T(8,128)(2,1)}, u32[]{:S(2)}) copy-start(bf16[16,16512]{1,0:T(8,128)(2,1)} %param.11) | copy-start | bytes 1585156
  58.6 1.2 %copy-start.1 = (f32[16,16512]{1,0:T(8,128)S(1)}, f32[16,16512]{1,0:T(8,128)}, u32[]{:S(2)}) copy-start(f32[16,16512]{1,0:T(8,128)} %fusion) | copy-start | bytes 3170308
  59.8 2.8 %copy-start.2 = (f32[16,16512]{1,0:T(8,128)S(1)}, f32[16,16512]{1,0:T(8,128)}, u32[]{:S(2)}) copy-start(f32[16,16512]{1,0:T(8,128)} %fusion) | copy-start | bytes 3170308
where the time goes:
time: 75.4 us; the launch traced here: 75 us
  blocking collectives  16.6 us (22%)
  waiting for transfers between devices  16.2 us (21%)
  other arithmetic  13.5 us (18%)
  starting transfers between devices  11.1 us (15%)
  matrix products  10.1 us (13%)
  local copies, waits for them, and re-layouts  6.68 us (9%)
    all_to_all x1, waiting for transfers between devices, local(): lax.all_to_all(outgoing[0], 'orient', split_axis=0, concat_axis=0, tiled=...  16.1 us
    all_gather x1, blocking collectives, local(): every_class = lax.all_gather(references, 'cls', axis=0, tiled=True)  8.49 us
    all_to_all x1, blocking collectives, local(): lax.all_to_all(shaped, 'orient', split_axis=0, concat_axis=0, tiled=True)  8.1 us
    all_to_all x1, starting transfers between devices, local(): lax.all_to_all(outgoing[1], 'orient', split_axis=0, concat_axis=0, tiled=...  6.32 us
    dot_general x2, matrix products, class_evidence(): lax.dot_general(weighted, shifted, (((1,), (1,)), ((), ())), preferred_el...  4.82 us
    all_to_all x1, starting transfers between devices, local(): lax.all_to_all(outgoing[0], 'orient', split_axis=0, concat_axis=0, tiled=...  4.81 us
    another operation x1, other arithmetic  3.64 us
    dot_general x2, matrix products, power_of(): lax.dot_general(table_squares, energy, (((1,), (1,)), ((), ())), precisio...  2.77 us
  transfers between devices with their start and end apart: 2, of which 1 were waited for; matrix products, arithmetic and copies ran while one was open for 21% of the time, Pallas kernels for 0%

commit v1 on v0

v1 whole, which is shorter than its diff:
```python
import functools
import math

import jax
import jax.numpy as jnp
from jax import lax
from jax.experimental import pallas as pl
from jax.experimental.pallas import tpu as pltpu
from jax.sharding import PartitionSpec as P

BOX = 256
KX = 129
KY = 128
EPSILON = 1e-06
LANES = 128
MESH = pl.DeviceIdType.MESH
HIGHEST = lax.Precision.HIGHEST
NT = (((1,), (1,)), ((), ()))


def repeat(count, body):
    if count <= 8:
        for step in range(count):
            body(step)
    else:
        pl.loop(0, count)(body)


def sine(quarter):
    x = quarter * (math.pi / 128)
    s = x * x
    p = -2.5052108e-08
    p = p * s + 2.7557319e-06
    p = p * s - 1.9841270e-04
    p = p * s + 8.3333333e-03
    p = p * s - 1.6666667e-01
    return x + x * (s * p)


def kernel(
    zs, xs, blocks, listed, shifts, codes, rows, pixels, wide,
    index_ref, sig_ref, off_ref, beta_ref, part_hbm, table_hbm, refs_hbm,
    post_ref, log_ref,
    land, part, table, ctf, shifted, rsq, csq, tp, acc, power,
    in_sem, land_sem, sib_sem, tp_sem, zsend, xsend, sibsend, tpsend,
):
    z, x, h = lax.axis_index("orient"), lax.axis_index("cls"), lax.axis_index("dom")
    peers = zs * xs
    me = x * zs + z
    half = wide // 2
    tiles = pixels // LANES
    mine = pl.ds(pl.multiple_of(h * half, LANES), half)
    theirs = pl.ds(pl.multiple_of((1 - h) * half, LANES), half)
    barrier = pltpu.get_barrier_semaphore()

    def peer(offset):
        number = lax.rem(me + offset, peers)
        return {"orient": lax.rem(number, zs), "cls": lax.div(number, zs)}

    @functools.partial(repeat, peers - 1)
    def _(i):
        pl.semaphore_signal(barrier, inc=1, device_id=peer(i + 1), device_id_type=MESH)

    pl.semaphore_signal(barrier, inc=1, device_id={"dom": 1 - h}, device_id_type=MESH)
    loads = [
        pltpu.make_async_copy(part_hbm, part, in_sem.at[0]),
        pltpu.make_async_copy(table_hbm, table, in_sem.at[1]),
        pltpu.make_async_copy(refs_hbm, land.at[x, z], in_sem.at[2]),
    ]
    for load in loads:
        load.start()
    pl.semaphore_wait(barrier, peers)

    def z_copy(zz, direction, src):
        return pltpu.make_async_remote_copy(
            src_ref=src, dst_ref=land.at[x, zz, :, mine],
            send_sem=zsend.at[direction, zz], recv_sem=land_sem.at[x, zz],
            device_id={"orient": z + 1 - 2 * direction}, device_id_type=MESH,
        )

    def x_copy(c, zz, direction, src):
        return pltpu.make_async_remote_copy(
            src_ref=src, dst_ref=land.at[c, zz, :, mine],
            send_sem=xsend.at[direction, c, zz], recv_sem=land_sem.at[c, zz],
            device_id={"cls": x + 1 - 2 * direction}, device_id_type=MESH,
        )

    def sib_copy(c, zz):
        return pltpu.make_async_remote_copy(
            src_ref=land.at[c, zz, :, mine], dst_ref=land.at[c, zz, :, mine],
            send_sem=sibsend.at[c, zz], recv_sem=sib_sem.at[c, zz],
            device_id={"dom": 1 - h}, device_id_type=MESH,
        )

    def z_targets(zz):
        return (z < zs - 1) & (zz <= z), (z > 0) & (zz >= z)

    def x_targets(c):
        return (x < xs - 1) & (c <= x), (x > 0) & (c >= x)

    own = refs_hbm.at[:, mine]
    for direction, wanted in enumerate(z_targets(z)):
        pl.when(wanted)(lambda d=direction: z_copy(z, d, own).start())
    for direction, wanted in enumerate(x_targets(x)):
        pl.when(wanted)(lambda d=direction: x_copy(x, z, d, own).start())

    def landed(c, zz):
        pltpu.make_async_copy(land.at[c, zz, :, mine], land.at[c, zz, :, mine], land_sem.at[c, zz]).wait()

    def from_z(zz):
        landed(x, zz)
        src = land.at[x, zz, :, mine]
        for direction, wanted in enumerate(z_targets(zz)):
            pl.when(wanted)(lambda d=direction: z_copy(zz, d, src).start())
        for direction, wanted in enumerate(x_targets(x)):
            pl.when(wanted)(lambda d=direction: x_copy(x, zz, d, src).start())
        sib_copy(x, zz).start()

    def z_step(step):
        for zz in (z - step - 1, z + step + 1):
            pl.when((zz >= 0) & (zz < zs))(lambda zz=zz: from_z(zz))

    def from_x(c, zz):
        landed(c, zz)
        src = land.at[c, zz, :, mine]
        for direction, wanted in enumerate(x_targets(c)):
            pl.when(wanted)(lambda d=direction: x_copy(c, zz, d, src).start())
        sib_copy(c, zz).start()

    def x_step(step, zstep):
        for c in (x - step - 1, x + step + 1):
            for zz in (z - zstep, z + zstep) if not (isinstance(zstep, int) and zstep == 0) else (z,):
                pl.when((c >= 0) & (c < xs) & (zz >= 0) & (zz < zs))(lambda c=c, zz=zz: from_x(c, zz))

    row = lax.broadcasted_iota(jnp.int32, (rows, 1), 0)
    lane = lax.broadcasted_iota(jnp.int32, (1, LANES), 1)

    code_of = jnp.zeros((rows, codes), jnp.int32)
    row_codes = lax.broadcasted_iota(jnp.int32, (rows, codes), 0) // 2
    for p in range(rows // 2):
        code_of = jnp.where(row_codes == p, index_ref[p], code_of)
    choice = (code_of == lax.broadcasted_iota(jnp.int32, (rows, codes), 1)).astype(jnp.float32)

    for load in loads:
        load.wait()

    @pl.loop(0, tiles)
    def _(k):
        at = pl.ds(pl.multiple_of(k * LANES, LANES), LANES)
        r = land[x, z, :, at].astype(jnp.float32)
        r = r * r
        high = r.astype(jnp.bfloat16).astype(jnp.float32)
        rsq[:, at] = jnp.concatenate([high, r - high], axis=0).astype(jnp.bfloat16)
        c = table[:, at].astype(jnp.float32)
        c = c * c
        high = c.astype(jnp.bfloat16).astype(jnp.float32)
        csq[:, at] = jnp.concatenate([high, c - high], axis=0).astype(jnp.bfloat16)

    products = lax.dot_general(csq[...], rsq[...], NT, preferred_element_type=jnp.float32)
    products = products[:codes] + products[codes:]
    eight = land.shape[2]
    products = products[:, :eight] + products[:, eight:]
    spread = jnp.concatenate([products, jnp.zeros((codes, LANES - eight), jnp.float32)], axis=1)
    tp[x, z] = pltpu.roll(spread, z * eight, 1)

    def tp_copy(offset):
        return pltpu.make_async_remote_copy(
            src_ref=tp.at[x, z], dst_ref=tp.at[x, z],
            send_sem=tpsend.at[offset], recv_sem=tp_sem.at[x, z],
            device_id=peer(offset), device_id_type=MESH,
        )

    repeat(peers - 1, lambda i: tp_copy(i + 1).start())

    ctf[...] = jnp.dot(
        choice.astype(jnp.bfloat16), table[...], preferred_element_type=jnp.float32
    ).astype(jnp.bfloat16)
    z_step(0)

    trow = lax.broadcasted_iota(jnp.int32, (8, LANES), 0)
    tx = jnp.zeros((8, LANES), jnp.int32)
    ty = jnp.zeros((8, LANES), jnp.int32)
    for t in range(shifts):
        tx = jnp.where(trow == t, off_ref[t, 0], tx)
        ty = jnp.where(trow == t, off_ref[t, 1], ty)
    lanes8 = lax.broadcasted_iota(jnp.int32, (8, LANES), 1)
    odd = (lax.broadcasted_iota(jnp.int32, (rows, LANES), 0) % 2) == 1
    power[...] = jnp.zeros_like(power)
    if wide > pixels:
        shifted[:, pl.ds(pixels, wide - pixels)] = jnp.zeros((shifts * rows, wide - pixels), jnp.bfloat16)

    def turn(k):
        at = pl.ds(pl.multiple_of(k * LANES, LANES), LANES)
        j = lanes8 + k * LANES
        line = ((j.astype(jnp.float32) + 0.5) * (1.0 / KX)).astype(jnp.int32)
        m = (tx * (j - line * KX) + ty * (line - KY // 2)) & (BOX - 1)
        m = m.astype(jnp.float32)
        fold = BOX // 4 - jnp.abs(m - BOX // 2)
        sines = sine(jnp.where(m < BOX // 2, 1.0, -1.0) * (BOX // 4 - jnp.abs(BOX // 4 - jnp.where(m < BOX // 2, m, m - BOX // 2))))
        cosines = -sine(fold)
        image = part[:, at].astype(jnp.float32)
        power[...] += image * image
        w = (image * ctf[:, at].astype(jnp.float32)).astype(jnp.bfloat16).astype(jnp.float32)
        other = jnp.where(odd, pltpu.roll(w, 1, 0), -pltpu.roll(w, rows - 1, 0))
        for t in range(shifts):
            turned = w * cosines[t:t + 1] + other * sines[t:t + 1]
            shifted[pl.ds(t * rows, rows), at] = turned.astype(jnp.bfloat16)

    stages = 3
    cuts = [tiles * i // stages for i in range(stages + 1)]

    def turns(stage):
        pl.loop(cuts[stage], cuts[stage + 1])(turn)

    turns(0)
    repeat_from = functools.partial(x_step, 0)
    repeat_from(0)
    if zs > 2:
        z_step(1)
    turns(1)
    repeat_from(1)
    turns(2)
    if zs > 3:
        z_step(2)
    if zs > 4:
        pl.loop(3, zs - 1)(z_step)
    if zs > 2:
        pl.loop(2, zs)(repeat_from)
    for step in range(1, xs - 1):
        x_step(step, 0)
        pl.loop(1, zs)(functools.partial(x_step, step))

    def everyone(i):
        c, zz = lax.div(i, zs), lax.rem(i, zs)

        @pl.when(i != me)
        def _():
            dst = land.at[c, zz, :, theirs]
            pltpu.make_async_copy(dst, dst, sib_sem.at[c, zz]).wait()
            pltpu.make_async_copy(tp.at[c, zz], tp.at[c, zz], tp_sem.at[c, zz]).wait()

    repeat(peers, everyone)

    image_power = jnp.sum(power[...], axis=1, keepdims=True)
    image_power = image_power + jnp.where(row % 2 == 1, pltpu.roll(jnp.broadcast_to(image_power, (rows, LANES)), 1, 0), pltpu.roll(jnp.broadcast_to(image_power, (rows, LANES)), rows - 1, 0))
    beta_lane = lax.broadcasted_iota(jnp.int32, (rows, rows // 2), 1)
    beta_row = lax.broadcasted_iota(jnp.int32, (rows, rows // 2), 0) // 2
    beta = jnp.sum(jnp.where(beta_lane == beta_row, beta_ref[...].astype(jnp.float32), 0.0), axis=1, keepdims=True)
    member = jnp.zeros((rows, LANES), jnp.bool_)
    group = lax.broadcasted_iota(jnp.int32, (rows, LANES), 1) // eight
    block = lax.broadcasted_iota(jnp.int32, (rows, LANES), 0) // (rows // blocks)
    for b in range(blocks):
        for s in range(listed):
            member = member | ((block == b) & (group == sig_ref[b, s]))
    lane_all = lax.broadcasted_iota(jnp.int32, (rows, LANES), 1)
    member = member & (lane_all % 2 == 0) & (lane_all < zs * eight)
    step_k = wide
    for parts in (5, 13):
        if step_k % (parts * 256) == 0 and step_k > 3328:
            step_k = wide // parts
    acc[...] = jnp.zeros_like(acc)
    evidence = jnp.zeros((rows, LANES), jnp.float32)
    for c in range(xs):
        def dots(i, total):
            at = pl.ds(pl.multiple_of(i * step_k, LANES), step_k)
            refs = land[c, :, :, at].reshape(zs * eight, step_k)
            return total + lax.dot_general(shifted[:, at], refs, NT, preferred_element_type=jnp.float32)

        total = lax.fori_loop(0, wide // step_k, dots, jnp.zeros((shifts * rows, zs * eight), jnp.float32))
        acc[:, pl.ds(0, zs * eight)] = total
        both = acc[...]
        arow = lax.broadcasted_iota(jnp.int32, both.shape, 0)
        acol = lax.broadcasted_iota(jnp.int32, both.shape, 1)
        both = jnp.where(arow % 2 == acol % 2, both, 0.0)
        both = both + pltpu.roll(both, shifts * rows - 1, 0)
        both = both + pltpu.roll(both, LANES - 1, 1)
        table_power = tp[c, 0]
        for zz in range(1, zs):
            table_power = table_power + tp[c, zz]
        ref_power = jnp.dot(choice, table_power, precision=HIGHEST, preferred_element_type=jnp.float32)
        ref_power = ref_power + pltpu.roll(ref_power, LANES - 1, 1)
        scale = beta / jnp.sqrt(image_power * ref_power + EPSILON)
        summed = jnp.zeros((rows, LANES), jnp.float32)
        for t in range(shifts):
            summed = summed + jnp.exp(both[t * rows:(t + 1) * rows] * scale)
        found = jnp.sum(jnp.where(member, summed, 0.0), axis=1, keepdims=True)
        evidence = jnp.where(lane_all == c, found, evidence)

    half_rows = rows // 2
    pick = (
        lax.broadcasted_iota(jnp.int32, (half_rows, rows), 1)
        == 2 * lax.broadcasted_iota(jnp.int32, (half_rows, rows), 0)
    ).astype(jnp.float32)
    evidence = jnp.dot(pick, jnp.where(odd, 0.0, evidence), precision=HIGHEST, preferred_element_type=jnp.float32)
    total = jnp.sum(evidence, axis=1, keepdims=True)
    post_ref[...] = (evidence / total)[:, :xs]
    diagonal = lax.broadcasted_iota(jnp.int32, (half_rows, half_rows), 0) == lax.broadcasted_iota(
        jnp.int32, (half_rows, half_rows), 1
    )
    log_ref[...] = jnp.sum(jnp.where(diagonal, jnp.log(total), 0.0), axis=0, keepdims=True)

    def sent(i):
        c, zz = lax.div(i, zs), lax.rem(i, zs)
        pl.when(i != me)(lambda: sib_copy(c, zz).wait_send())

        @pl.when(c == x)
        def _():
            for direction, wanted in enumerate(z_targets(zz)):
                pl.when(wanted)(lambda d=direction: z_copy(zz, d, own).wait_send())

        for direction, wanted in enumerate(x_targets(c)):
            pl.when(wanted)(lambda d=direction: x_copy(c, zz, d, own).wait_send())

    repeat(peers, sent)
    repeat(peers - 1, lambda i: tp_copy(i + 1).wait_send())


def local(particles, ctf_index, beta, significant, ctf_table, references, offsets):
    zs, xs = lax.axis_size("orient"), lax.axis_size("cls")
    count, _, pixels = particles.shape
    orients = references.shape[2]
    eight, rows = 2 * orients, 2 * count
    codes = ctf_table.shape[0]
    shifts = offsets.shape[0]
    wide = -(-pixels // 256) * 256
    refs = jnp.pad(references.reshape(eight, pixels), ((0, 0), (0, wide - pixels)))
    parts = particles.reshape(rows, pixels)
    smem = pl.BlockSpec(memory_space=pltpu.SMEM)
    vmem = pl.BlockSpec(memory_space=pltpu.VMEM)
    anywhere = pl.BlockSpec(memory_space=pl.ANY)
    dma = pltpu.SemaphoreType.DMA
    post, logs = pl.pallas_call(
        functools.partial(
            kernel, zs, xs, significant.shape[0], significant.shape[1], shifts, codes, rows, pixels, wide
        ),
        out_shape=(
            jax.ShapeDtypeStruct((count, xs), jnp.float32),
            jax.ShapeDtypeStruct((1, count), jnp.float32),
        ),
        in_specs=[smem, smem, smem, vmem, anywhere, anywhere, anywhere],
        out_specs=(vmem, vmem),
        scratch_shapes=[
            pltpu.VMEM((xs, zs, eight, wide), jnp.bfloat16),
            pltpu.VMEM((rows, pixels), jnp.bfloat16),
            pltpu.VMEM((codes, pixels), jnp.bfloat16),
            pltpu.VMEM((rows, pixels), jnp.bfloat16),
            pltpu.VMEM((shifts * rows, wide), jnp.bfloat16),
            pltpu.VMEM((2 * eight, pixels), jnp.bfloat16),
            pltpu.VMEM((2 * codes, pixels), jnp.bfloat16),
            pltpu.VMEM((xs, zs, codes, LANES), jnp.float32),
            pltpu.VMEM((shifts * rows, LANES), jnp.float32),
            pltpu.VMEM((rows, LANES), jnp.float32),
            dma((3,)),
            dma((xs, zs)),
            dma((xs, zs)),
            dma((xs, zs)),
            dma((2, zs)),
            dma((2, xs, zs)),
            dma((xs, zs)),
            dma((xs * zs,)),
        ],
        compiler_params=pltpu.CompilerParams(
            collective_id=0, has_side_effects=True, vmem_limit_bytes=58 * 2**20
        ),
    )(ctf_index, significant, offsets, beta.reshape(1, count), parts, ctf_table, refs)
    return post, logs.reshape(count)


def solution(mesh):
    everyone = ("groups", "orient", "cls", "dom")
    return jax.shard_map(
        local,
        mesh=mesh,
        in_specs=(
            P(everyone, None, None),
            P(everyone),
            P(everyone),
            P(everyone, None),
            P(),
            P(("groups", "cls"), "orient", None, None, None),
            P("groups", None),
        ),
        out_specs=(P(everyone, None), P(everyone)),
        check_vma=False,
    )
```

time: 75.4 us -> 38.1 us (0.51)
  the two profiles are of different devices: /device:TPU:0 before, /device:TPU:1 now
where the time goes in v1:
time: 38.1 us; the launch traced here: 37.9 us
  Pallas kernels  29.9 us (78%)
  local copies, waits for them, and re-layouts  7.32 us (19%)
  between operations  0.66 us (2%)
    pallas_call x1, Pallas kernels, local(): pl.pallas_call(functools.partial(kernel, zs, xs, significant.shape[0], si...  29.9 us
    unnamed x12, local copies, waits for them, and re-layouts  4.49 us
    reshape x1, local copies, waits for them, and re-layouts, local(): references.reshape(eight, pixels)  1.11 us
    reshape x1, local copies, waits for them, and re-layouts, local(): parts = particles.reshape(rows, pixels)  1 us

profile of v1, /device:TPU:1, one launch (start us, length us, event | category | flops | bytes accessed | tf_op | source)
XLA Modules:
  0.0 37.9 jit_solution(7955064759566038759)
XLA Ops:
  0.6 0.0 copy-start.2
  0.6 0.6 %copy-done.2 = s32[4,1]{0,1:T(1,128)S(1)} copy-done((s32[4,1]{0,1:T(1,128)S(1)}, s32[4,1]{0,1:T(1,128)}, u32[]{:S(2)}) %copy-start.2) | copy-done | bytes 40
  1.3 0.0 copy-start.1
  1.3 0.7 %copy.9.sig_ref = s32[4,1]{1,0:T(4,128)} copy(s32[4,1]{0,1:T(1,128)S(1)} %copy-done.2) | data formatting | bytes 32 | tf_op args[3]
  2.0 0.0 copy-done.1
  2.0 0.7 %copy.10.off_ref = s32[5,2]{1,0:T(8,128)} copy(s32[5,2]{0,1:T(2,128)S(1)} %copy-done.1) | data formatting | bytes 80 | tf_op args[6]
  2.6 0.0 copy-start
  2.6 1.1 %reshape.18 = bf16[8,16512]{1,0:T(8,128)(2,1)S(1)} reshape(bf16[1,1,4,2,16512]{4,3,2,1,0:T(2,128)(2,1)} %param.12) | data formatting | bytes 528384 | tf_op jit(solution)/shard_map/reshape | solution.py:326
  3.8 0.7 %pad.4.refs_hbm = bf16[8,16640]{1,0:T(8,128)(2,1)} pad(bf16[8,16512]{1,0:T(8,128)(2,1)S(1)} %reshape.18, bf16[]{:T(256)} %constant.2.clone.1), padding=0_0x0_128 | pad | bytes 530434 | tf_op jit(solution)/shard_map/jit(_pad)/pad | solution.py:326
  4.5 0.0 copy-done
  4.5 1.0 %reshape.17.part_hbm = bf16[16,16512]{1,0:T(8,128)(2,1)} reshape(bf16[8,2,16512]{2,1,0:T(2,128)(2,1)S(1)} %copy-done) | data formatting | bytes 1056768 | tf_op jit(solution)/shard_map/reshape | solution.py:327
  5.5 29.9 %shard_map.86 = (f32[8,2]{1,0:T(8,128)}, f32[1,8]{1,0:T(1,128)}) custom-call(s32[8]{0:T(128)} %index_ref.1, s32[4,1]{1,0:T(4,128)} %copy.9.sig_ref, s32[5,2]{1,0:T(8,128)} %copy.10.off_ref, bf16[1,8]{1,0:T(2,128)(2,1)} %bitcast.2, bf16[16,16512]{1,0:T(8,128)(2,1)} %reshape.17.part_hbm, bf16[16,16512]{1,0:T(8,128)(2,1)} %table_hbm.1, ...), custom_call_target="tpu_custom_call" | custom-call | tf_op jit(solution)/shard_map/pallas_call | solution.py:332
  35.4 1.3 %copy.11 = f32[8,2]{0,1:T(2,128)} copy(f32[8,2]{1,0:T(8,128)} %get-tuple-element.6) | data formatting | bytes 128
  36.7 0.0 copy-start.3
  36.7 0.7 %copy-done.3 = f32[1,8]{1,0:T(1,128)S(1)} copy-done((f32[1,8]{1,0:T(1,128)S(1)}, f32[1,8]{1,0:T(1,128)}, u32[]{:S(2)}) %copy-start.3) | copy-done | bytes 56
  37.4 0.5 %copy.13 = f32[8]{0:T(128)} copy(f32[8]{0:T(128)S(1)} %bitcast.3) | data formatting | bytes 64
Async XLA Ops:
  0.6 0.7 %copy-start.2 = (s32[4,1]{0,1:T(1,128)S(1)}, s32[4,1]{0,1:T(1,128)}, u32[]{:S(2)}) copy-start(s32[4,1]{0,1:T(1,128)} %param.10) | copy-start | bytes 52
  1.3 0.7 %copy-start.1 = (s32[5,2]{0,1:T(2,128)S(1)}, s32[5,2]{0,1:T(2,128)}, u32[]{:S(2)}) copy-start(s32[5,2]{0,1:T(2,128)} %param.13) | copy-start | bytes 124
  2.6 1.9 %copy-start = (bf16[8,2,16512]{2,1,0:T(2,128)(2,1)S(1)}, bf16[8,2,16512]{2,1,0:T(2,128)(2,1)}, u32[]{:S(2)}) copy-start(bf16[8,2,16512]{2,1,0:T(2,128)(2,1)} %param.7) | copy-start | bytes 1585156
  36.7 0.7 %copy-start.3 = (f32[1,8]{1,0:T(1,128)S(1)}, f32[1,8]{1,0:T(1,128)}, u32[]{:S(2)}) copy-start(f32[1,8]{1,0:T(1,128)} %get-tuple-element.5) | copy-start | bytes 100

commit v2 on v1

--- a/solution.py
+++ b/solution.py
@@ -38,19 +38,20 @@
 
 
 def kernel(
-    zs, xs, blocks, listed, shifts, codes, rows, pixels, wide,
+    zs, xs, blocks, listed, shifts, codes, rows, pixels,
     index_ref, sig_ref, off_ref, beta_ref, part_hbm, table_hbm, refs_hbm,
-    post_ref, log_ref,
-    land, part, table, ctf, shifted, rsq, csq, tp, acc, power,
+    out_ref,
+    part3, land, table, ctf, shifted, rsq, csq, tp, acc, power,
     in_sem, land_sem, sib_sem, tp_sem, zsend, xsend, sibsend, tpsend,
 ):
     z, x, h = lax.axis_index("orient"), lax.axis_index("cls"), lax.axis_index("dom")
     peers = zs * xs
+    eight = 2 * land.shape[2]
     me = x * zs + z
-    half = wide // 2
+    half = land.shape[2] // 2
     tiles = pixels // LANES
-    mine = pl.ds(pl.multiple_of(h * half, LANES), half)
-    theirs = pl.ds(pl.multiple_of((1 - h) * half, LANES), half)
+    mine = pl.ds(h * half, half)
+    theirs = pl.ds((1 - h) * half, half)
     barrier = pltpu.get_barrier_semaphore()
 
     def peer(offset):
@@ -63,7 +64,7 @@
 
     pl.semaphore_signal(barrier, inc=1, device_id={"dom": 1 - h}, device_id_type=MESH)
     loads = [
-        pltpu.make_async_copy(part_hbm, part, in_sem.at[0]),
+        pltpu.make_async_copy(part_hbm, part3, in_sem.at[0]),
         pltpu.make_async_copy(table_hbm, table, in_sem.at[1]),
         pltpu.make_async_copy(refs_hbm, land.at[x, z], in_sem.at[2]),
     ]
@@ -73,21 +74,21 @@
 
     def z_copy(zz, direction, src):
         return pltpu.make_async_remote_copy(
-            src_ref=src, dst_ref=land.at[x, zz, :, mine],
+            src_ref=src, dst_ref=land.at[x, zz, mine],
             send_sem=zsend.at[direction, zz], recv_sem=land_sem.at[x, zz],
             device_id={"orient": z + 1 - 2 * direction}, device_id_type=MESH,
         )
 
     def x_copy(c, zz, direction, src):
         return pltpu.make_async_remote_copy(
-            src_ref=src, dst_ref=land.at[c, zz, :, mine],
+            src_ref=src, dst_ref=land.at[c, zz, mine],
             send_sem=xsend.at[direction, c, zz], recv_sem=land_sem.at[c, zz],
             device_id={"cls": x + 1 - 2 * direction}, device_id_type=MESH,
         )
 
     def sib_copy(c, zz):
         return pltpu.make_async_remote_copy(
-            src_ref=land.at[c, zz, :, mine], dst_ref=land.at[c, zz, :, mine],
+            src_ref=land.at[c, zz, mine], dst_ref=land.at[c, zz, mine],
             send_sem=sibsend.at[c, zz], recv_sem=sib_sem.at[c, zz],
             device_id={"dom": 1 - h}, device_id_type=MESH,
         )
@@ -98,18 +99,18 @@
     def x_targets(c):
         return (x < xs - 1) & (c <= x), (x > 0) & (c >= x)
 
-    own = refs_hbm.at[:, mine]
+    own = refs_hbm.at[mine]
     for direction, wanted in enumerate(z_targets(z)):
         pl.when(wanted)(lambda d=direction: z_copy(z, d, own).start())
     for direction, wanted in enumerate(x_targets(x)):
         pl.when(wanted)(lambda d=direction: x_copy(x, z, d, own).start())
 
     def landed(c, zz):
-        pltpu.make_async_copy(land.at[c, zz, :, mine], land.at[c, zz, :, mine], land_sem.at[c, zz]).wait()
+        pltpu.make_async_copy(land.at[c, zz, mine], land.at[c, zz, mine], land_sem.at[c, zz]).wait()
 
     def from_z(zz):
         landed(x, zz)
-        src = land.at[x, zz, :, mine]
+        src = land.at[x, zz, mine]
         for direction, wanted in enumerate(z_targets(zz)):
             pl.when(wanted)(lambda d=direction: z_copy(zz, d, src).start())
         for direction, wanted in enumerate(x_targets(x)):
@@ -122,7 +123,7 @@
 
     def from_x(c, zz):
         landed(c, zz)
-        src = land.at[c, zz, :, mine]
+        src = land.at[c, zz, mine]
         for direction, wanted in enumerate(x_targets(c)):
             pl.when(wanted)(lambda d=direction: x_copy(c, zz, d, src).start())
         sib_copy(c, zz).start()
@@ -147,7 +148,7 @@
     @pl.loop(0, tiles)
     def _(k):
         at = pl.ds(pl.multiple_of(k * LANES, LANES), LANES)
-        r = land[x, z, :, at].astype(jnp.float32)
+        r = land[x, z, :, :, at].reshape(eight, LANES).astype(jnp.float32)
         r = r * r
         high = r.astype(jnp.bfloat16).astype(jnp.float32)
         rsq[:, at] = jnp.concatenate([high, r - high], axis=0).astype(jnp.bfloat16)
@@ -158,7 +159,6 @@
 
     products = lax.dot_general(csq[...], rsq[...], NT, preferred_element_type=jnp.float32)
     products = products[:codes] + products[codes:]
-    eight = land.shape[2]
     products = products[:, :eight] + products[:, eight:]
     spread = jnp.concatenate([products, jnp.zeros((codes, LANES - eight), jnp.float32)], axis=1)
     tp[x, z] = pltpu.roll(spread, z * eight, 1)
@@ -181,13 +181,11 @@
     tx = jnp.zeros((8, LANES), jnp.int32)
     ty = jnp.zeros((8, LANES), jnp.int32)
     for t in range(shifts):
-        tx = jnp.where(trow == t, off_ref[t, 0], tx)
-        ty = jnp.where(trow == t, off_ref[t, 1], ty)
+        tx = jnp.where(trow == t, off_ref[0, t], tx)
+        ty = jnp.where(trow == t, off_ref[1, t], ty)
     lanes8 = lax.broadcasted_iota(jnp.int32, (8, LANES), 1)
     odd = (lax.broadcasted_iota(jnp.int32, (rows, LANES), 0) % 2) == 1
     power[...] = jnp.zeros_like(power)
-    if wide > pixels:
-        shifted[:, pl.ds(pixels, wide - pixels)] = jnp.zeros((shifts * rows, wide - pixels), jnp.bfloat16)
 
     def turn(k):
         at = pl.ds(pl.multiple_of(k * LANES, LANES), LANES)
@@ -198,7 +196,7 @@
         fold = BOX // 4 - jnp.abs(m - BOX // 2)
         sines = sine(jnp.where(m < BOX // 2, 1.0, -1.0) * (BOX // 4 - jnp.abs(BOX // 4 - jnp.where(m < BOX // 2, m, m - BOX // 2))))
         cosines = -sine(fold)
-        image = part[:, at].astype(jnp.float32)
+        image = part3[:, :, at].reshape(rows, LANES).astype(jnp.float32)
         power[...] += image * image
         w = (image * ctf[:, at].astype(jnp.float32)).astype(jnp.bfloat16).astype(jnp.float32)
         other = jnp.where(odd, pltpu.roll(w, 1, 0), -pltpu.roll(w, rows - 1, 0))
@@ -224,22 +222,16 @@
         z_step(2)
     if zs > 4:
         pl.loop(3, zs - 1)(z_step)
-    if zs > 2:
-        pl.loop(2, zs)(repeat_from)
-    for step in range(1, xs - 1):
-        x_step(step, 0)
-        pl.loop(1, zs)(functools.partial(x_step, step))
-
-    def everyone(i):
-        c, zz = lax.div(i, zs), lax.rem(i, zs)
-
-        @pl.when(i != me)
+    if zs > 3:
+        pl.loop(2, zs - 1)(repeat_from)
+
+    def complete(c, zz):
+
+        @pl.when((c != x) | (zz != z))
         def _():
-            dst = land.at[c, zz, :, theirs]
+            dst = land.at[c, zz, theirs]
             pltpu.make_async_copy(dst, dst, sib_sem.at[c, zz]).wait()
             pltpu.make_async_copy(tp.at[c, zz], tp.at[c, zz], tp_sem.at[c, zz]).wait()
-
-    repeat(peers, everyone)
 
     image_power = jnp.sum(power[...], axis=1, keepdims=True)
     image_power = image_power + jnp.where(row % 2 == 1, pltpu.roll(jnp.broadcast_to(image_power, (rows, LANES)), 1, 0), pltpu.roll(jnp.broadcast_to(image_power, (rows, LANES)), rows - 1, 0))
@@ -251,22 +243,19 @@
     block = lax.broadcasted_iota(jnp.int32, (rows, LANES), 0) // (rows // blocks)
     for b in range(blocks):
         for s in range(listed):
-            member = member | ((block == b) & (group == sig_ref[b, s]))
+            member = member | ((block == b) & (group == sig_ref[b * listed + s]))
     lane_all = lax.broadcasted_iota(jnp.int32, (rows, LANES), 1)
     member = member & (lane_all % 2 == 0) & (lane_all < zs * eight)
-    step_k = wide
-    for parts in (5, 13):
-        if step_k % (parts * 256) == 0 and step_k > 3328:
-            step_k = wide // parts
     acc[...] = jnp.zeros_like(acc)
-    evidence = jnp.zeros((rows, LANES), jnp.float32)
-    for c in range(xs):
+    step_k = next(pixels // n for n in (3, 5, 1) if tiles % n == 0)
+
+    def score(c, evidence):
         def dots(i, total):
             at = pl.ds(pl.multiple_of(i * step_k, LANES), step_k)
-            refs = land[c, :, :, at].reshape(zs * eight, step_k)
+            refs = land[c, :, :, :, at].reshape(zs * eight, step_k)
             return total + lax.dot_general(shifted[:, at], refs, NT, preferred_element_type=jnp.float32)
 
-        total = lax.fori_loop(0, wide // step_k, dots, jnp.zeros((shifts * rows, zs * eight), jnp.float32))
+        total = lax.fori_loop(0, pixels // step_k, dots, jnp.zeros((shifts * rows, zs * eight), jnp.float32))
         acc[:, pl.ds(0, zs * eight)] = total
         both = acc[...]
         arow = lax.broadcasted_iota(jnp.int32, both.shape, 0)
@@ -284,7 +273,19 @@
         for t in range(shifts):
             summed = summed + jnp.exp(both[t * rows:(t + 1) * rows] * scale)
         found = jnp.sum(jnp.where(member, summed, 0.0), axis=1, keepdims=True)
-        evidence = jnp.where(lane_all == c, found, evidence)
+        return jnp.where(lane_all == c, found, evidence)
+
+    repeat(zs, lambda zz: complete(x, zz))
+    evidence = score(x, jnp.zeros((rows, LANES), jnp.float32))
+    if zs > 2:
+        repeat_from(zs - 1)
+    for step in range(1, xs - 1):
+        x_step(step, 0)
+        pl.loop(1, zs)(functools.partial(x_step, step))
+    for i in range(1, xs):
+        c = lax.rem(x + i, xs)
+        repeat(zs, functools.partial(complete, c))
+        evidence = score(c, evidence)
 
     half_rows = rows // 2
     pick = (
@@ -292,12 +293,11 @@
         == 2 * lax.broadcasted_iota(jnp.int32, (half_rows, rows), 0)
     ).astype(jnp.float32)
     evidence = jnp.dot(pick, jnp.where(odd, 0.0, evidence), precision=HIGHEST, preferred_element_type=jnp.float32)
-    total = jnp.sum(evidence, axis=1, keepdims=True)
-    post_ref[...] = (evidence / total)[:, :xs]
     diagonal = lax.broadcasted_iota(jnp.int32, (half_rows, half_rows), 0) == lax.broadcasted_iota(
         jnp.int32, (half_rows, half_rows), 1
     )
-    log_ref[...] = jnp.sum(jnp.where(diagonal, jnp.log(total), 0.0), axis=0, keepdims=True)
+    for c in range(xs):
+        out_ref[c:c + 1, :] = jnp.sum(jnp.where(diagonal, evidence[:, c:c + 1], 0.0), axis=0, keepdims=True)
 
     def sent(i):
         c, zz = lax.div(i, zs), lax.rem(i, zs)
@@ -322,29 +322,25 @@
     eight, rows = 2 * orients, 2 * count
     codes = ctf_table.shape[0]
     shifts = offsets.shape[0]
-    wide = -(-pixels // 256) * 256
-    refs = jnp.pad(references.reshape(eight, pixels), ((0, 0), (0, wide - pixels)))
-    parts = particles.reshape(rows, pixels)
+    refs = references.reshape(orients, 2, pixels)
+    parts = particles
     smem = pl.BlockSpec(memory_space=pltpu.SMEM)
     vmem = pl.BlockSpec(memory_space=pltpu.VMEM)
     anywhere = pl.BlockSpec(memory_space=pl.ANY)
     dma = pltpu.SemaphoreType.DMA
-    post, logs = pl.pallas_call(
+    evidence = pl.pallas_call(
         functools.partial(
-            kernel, zs, xs, significant.shape[0], significant.shape[1], shifts, codes, rows, pixels, wide
+            kernel, zs, xs, significant.shape[0], significant.shape[1], shifts, codes, rows, pixels
         ),
-        out_shape=(
-            jax.ShapeDtypeStruct((count, xs), jnp.float32),
-            jax.ShapeDtypeStruct((1, count), jnp.float32),
-        ),
+        out_shape=jax.ShapeDtypeStruct((xs, count), jnp.float32),
         in_specs=[smem, smem, smem, vmem, anywhere, anywhere, anywhere],
-        out_specs=(vmem, vmem),
+        out_specs=vmem,
         scratch_shapes=[
-            pltpu.VMEM((xs, zs, eight, wide), jnp.bfloat16),
-            pltpu.VMEM((rows, pixels), jnp.bfloat16),
+            pltpu.VMEM((count, 2, pixels), jnp.bfloat16),
+            pltpu.VMEM((xs, zs, orients, 2, pixels), jnp.bfloat16),
             pltpu.VMEM((codes, pixels), jnp.bfloat16),
             pltpu.VMEM((rows, pixels), jnp.bfloat16),
-            pltpu.VMEM((shifts * rows, wide), jnp.bfloat16),
+            pltpu.VMEM((shifts * rows, pixels), jnp.bfloat16),
             pltpu.VMEM((2 * eight, pixels), jnp.bfloat16),
             pltpu.VMEM((2 * codes, pixels), jnp.bfloat16),
             pltpu.VMEM((xs, zs, codes, LANES), jnp.float32),
@@ -362,8 +358,9 @@
         compiler_params=pltpu.CompilerParams(
             collective_id=0, has_side_effects=True, vmem_limit_bytes=58 * 2**20
         ),
-    )(ctf_index, significant, offsets, beta.reshape(1, count), parts, ctf_table, refs)
-    return post, logs.reshape(count)
+    )(ctf_index, significant.reshape(-1), offsets.T, beta.reshape(1, count), parts, ctf_table, refs)
+    total = jnp.sum(evidence, axis=0)
+    return (evidence / total[None]).T, jnp.log(total)
 
 
 def solution(mesh):

time: 38.1 us -> 29.7 us (0.78)
  local copies, waits for them, and re-layouts: 7.32 us -> 0.52 us
  Pallas kernels: 29.9 us -> 27 us
  other arithmetic: 0 us -> 1.33 us
    unnamed x12 -> x2, local copies, waits for them, and re-layouts: 4.49 us -> 0.01 us
    pallas_call x1, Pallas kernels: 29.9 us -> 27 us  [local(): pl.pallas_call(functools.partial(kernel, zs, xs, significant.shape[0], si...]
    reshape x2 -> x0, local copies, waits for them, and re-layouts: 2.11 us -> none  [the longest x1 1.11 us: local(): references.reshape(eight, pixels)]
    reduce_sum x0 -> x1, other arithmetic: none -> 0.76 us  [local(): total = jnp.sum(evidence, axis=0)]
    pad x1 -> x0, local copies, waits for them, and re-layouts: 0.73 us -> none  [local(): jnp.pad(references.reshape(eight, pixels), ((0, 0), (0, wide - pixels)))]
    transpose x0 -> x1, other arithmetic: none -> 0.57 us  [local(): return ((evidence / total[None]).T, jnp.log(total))]
    log x0 -> x1, local copies, waits for them, and re-layouts: none -> 0.52 us  [local(): return ((evidence / total[None]).T, jnp.log(total))]
where the time goes in v2:
time: 29.7 us; the launch traced here: 29.5 us
  Pallas kernels  27 us (91%)
  other arithmetic  1.33 us (4%)
  between operations  0.65 us (2%)
  local copies, waits for them, and re-layouts  0.52 us (2%)
    pallas_call x1, Pallas kernels, local(): pl.pallas_call(functools.partial(kernel, zs, xs, significant.shape[0], si...  27 us
    reduce_sum x1, other arithmetic, local(): total = jnp.sum(evidence, axis=0)  0.76 us

profile of v2, /device:TPU:1, one launch (start us, length us, event | category | flops | bytes accessed | tf_op | source)
XLA Modules:
  0.0 29.5 jit_solution(11298230969827634877)
XLA Ops:
  0.6 27.0 %shard_map.86 = f32[2,8]{1,0:T(2,128)} custom-call(s32[8]{0:T(128)} %index_ref.1, s32[4]{0:T(128)} %bitcast.8, s32[2,5]{1,0:T(2,128)} %bitcast.7, bf16[1,8]{1,0:T(2,128)(2,1)} %bitcast.9, bf16[8,2,16512]{2,1,0:T(2,128)(2,1)} %part_hbm.1, bf16[16,16512]{1,0:T(8,128)(2,1)} %table_hbm.1, bf16[4,2,16512]{2,1,0:T(2,128)(2,1)} %bitcast.6), custom_call_target="tpu_custom_call" | custom-call | tf_op jit(solution)/shard_map/pallas_call | solution.py:331
  27.6 0.0 copy-start
  27.7 0.8 %reduce_sum.9 = f32[8]{0:T(128)S(1)} reduce(f32[2,8]{1,0:T(2,128)} %shard_map.86, f32[]{:T(128)} %constant.0.clone.1), dimensions={0}, to_apply=%region_0.0 | reduce | flops 8 | bytes 100 | tf_op jit(solution)/shard_map/reduce_sum | solution.py:362
  28.4 0.0 copy-done
  28.4 0.6 %divide_bitcast_fusion = f32[8,2]{0,1:T(2,128)} fusion(f32[2,8]{1,0:T(2,128)S(1)} %copy-done, f32[8]{0:T(128)S(1)} %reduce_sum.9), kind=kLoop, calls=%fused_computation | loop fusion | flops 16 | bytes 160 | tf_op jit(solution)/shard_map/transpose | solution.py:363
  29.0 0.5 %log.3 = f32[8]{0:T(128)} log(f32[8]{0:T(128)S(1)} %reduce_sum.9) | non-fusion elementwise | bytes 64 | tf_op jit(solution)/shard_map/log | solution.py:363
Async XLA Ops:
  27.6 0.8 %copy-start = (f32[2,8]{1,0:T(2,128)S(1)}, f32[2,8]{1,0:T(2,128)}, u32[]{:S(2)}) copy-start(f32[2,8]{1,0:T(2,128)} %shard_map.86) | copy-start | bytes 196

commit v3 on v2

--- a/solution.py
+++ b/solution.py
@@ -145,7 +145,7 @@
     for load in loads:
         load.wait()
 
-    @pl.loop(0, tiles)
+    @pl.loop(0, tiles, unroll=3)
     def _(k):
         at = pl.ds(pl.multiple_of(k * LANES, LANES), LANES)
         r = land[x, z, :, :, at].reshape(eight, LANES).astype(jnp.float32)
@@ -208,7 +208,7 @@
     cuts = [tiles * i // stages for i in range(stages + 1)]
 
     def turns(stage):
-        pl.loop(cuts[stage], cuts[stage + 1])(turn)
+        pl.loop(cuts[stage], cuts[stage + 1], unroll=2)(turn)
 
     turns(0)
     repeat_from = functools.partial(x_step, 0)

time: 29.7 us -> 29.4 us (0.990)
  Pallas kernels: 27 us -> 26.7 us
where the time goes in v3:
time: 29.4 us; the launch traced here: 29.2 us
  Pallas kernels  26.7 us (91%)
  other arithmetic  1.33 us (5%)
  between operations  0.65 us (2%)
  local copies, waits for them, and re-layouts  0.52 us (2%)
    pallas_call x1, Pallas kernels, local(): pl.pallas_call(functools.partial(kernel, zs, xs, significant.shape[0], si...  26.7 us
    reduce_sum x1, other arithmetic, local(): total = jnp.sum(evidence, axis=0)  0.76 us

profile of v3, /device:TPU:1, one launch (start us, length us, event | category | flops | bytes accessed | tf_op | source)
XLA Modules:
  0.0 29.2 jit_solution(12103315723606268182)
XLA Ops:
  0.6 26.7 %shard_map.86 = f32[2,8]{1,0:T(2,128)} custom-call(s32[8]{0:T(128)} %index_ref.1, s32[4]{0:T(128)} %bitcast.8, s32[2,5]{1,0:T(2,128)} %bitcast.7, bf16[1,8]{1,0:T(2,128)(2,1)} %bitcast.9, bf16[8,2,16512]{2,1,0:T(2,128)(2,1)} %part_hbm.1, bf16[16,16512]{1,0:T(8,128)(2,1)} %table_hbm.1, bf16[4,2,16512]{2,1,0:T(2,128)(2,1)} %bitcast.6), custom_call_target="tpu_custom_call" | custom-call | tf_op jit(solution)/shard_map/pallas_call | solution.py:331
  27.4 0.0 copy-start
  27.4 0.8 %reduce_sum.9 = f32[8]{0:T(128)S(1)} reduce(f32[2,8]{1,0:T(2,128)} %shard_map.86, f32[]{:T(128)} %constant.0.clone.1), dimensions={0}, to_apply=%region_0.0 | reduce | flops 8 | bytes 100 | tf_op jit(solution)/shard_map/reduce_sum | solution.py:362
  28.1 0.0 copy-done
  28.1 0.6 %divide_bitcast_fusion = f32[8,2]{0,1:T(2,128)} fusion(f32[2,8]{1,0:T(2,128)S(1)} %copy-done, f32[8]{0:T(128)S(1)} %reduce_sum.9), kind=kLoop, calls=%fused_computation | loop fusion | flops 16 | bytes 160 | tf_op jit(solution)/shard_map/transpose | solution.py:363
  28.7 0.5 %log.3 = f32[8]{0:T(128)} log(f32[8]{0:T(128)S(1)} %reduce_sum.9) | non-fusion elementwise | bytes 64 | tf_op jit(solution)/shard_map/log | solution.py:363
Async XLA Ops:
  27.4 0.8 %copy-start = (f32[2,8]{1,0:T(2,128)S(1)}, f32[2,8]{1,0:T(2,128)}, u32[]{:S(2)}) copy-start(f32[2,8]{1,0:T(2,128)} %shard_map.86) | copy-start | bytes 196
